TPU v7x, 512 devices: a whole 4x4x16 slice. The times are simulated.
512 devices in a mesh: prompt: 16 (over z), seq: 32 (over y, x, core).
Axes of the slice: x: 4, y: 4, z: 16, core: 2. Of those that a mesh axis runs over, the one named last changes fastest.
Arguments:
- queries: bfloat16 [16, 32, 2, 32, 128], P('prompt', 'seq'), may hold values from -160 to 160
- prompt_key_cache: bfloat16 [16, 4, 8192, 128], P('prompt', None, 'seq'), may hold values from -5 to 5
- prompt_value_cache: bfloat16 [16, 4, 8192, 128], P('prompt', None, 'seq'), may hold values from -6 to 6
- kept: int32 [16, 4, 32], P('prompt', None, 'seq'), may hold values from 1 to 2, as said below
- sample_keys: bfloat16 [16, 32, 4, 256, 128], P('prompt', 'seq'), may hold values from -6 to 6
- sample_values: bfloat16 [16, 32, 4, 256, 128], P('prompt', 'seq'), may hold values from -6 to 6
- suffix_len: int32 [16, 32], P('prompt', 'seq'), may hold values from 1 to 256, as said below
- decode_keys: bfloat16 [16, 32, 2, 4, 128], P('prompt', 'seq'), may hold values from -6 to 6
- decode_values: bfloat16 [16, 32, 2, 4, 128], P('prompt', 'seq'), may hold values from -6 to 6
- out_weight: bfloat16 [4096, 8192], P('seq', 'prompt'), may hold values from -0.1875 to 0.1875
Outputs:
- attn_out: bfloat16 [1024, 8192], P('seq', 'prompt')
Inputs may be any that keep to these rules, and one draw needn't show every extreme that they name: `kept`: for every prompt and key-value head some seq index has all 2 slots live. `suffix_len`: in every prompt some sample has 256 generated tokens.
All inputs are finite; a program needn't handle non-finite values.
Results may differ from a plain program's by a relative error of at most 0.0048.
Values may be sent and summed in bfloat16 or wider, within the bound.
A program may use at most 128 MiB of HBM per device.

v0:
```python
import math
import jax
import jax.numpy as jnp
from jax import lax
from jax.sharding import PartitionSpec as P

BLOCK_TOKENS = 128
KEPT_SLOTS = 2
NEGATIVE = -1e30


def joined(x, axis, combine):
    everything = jax.tree.map(lambda part: lax.all_gather(part, axis), x)
    initial = jax.tree.map(lambda part: part[0], everything)

    def lap(k, so_far):
        return combine(so_far, jax.tree.map(lambda part: part[k], everything))

    return lax.fori_loop(1, lax.axis_size(axis), lap, initial)


def combine(earlier, later):
    highest = jnp.maximum(earlier[0], later[0])
    early_factor = jnp.exp(earlier[0] - highest)
    late_factor = jnp.exp(later[0] - highest)
    softmax_total = earlier[1] * early_factor + later[1] * late_factor
    summed = earlier[2] * early_factor[..., None] + later[2] * late_factor[..., None]
    return (highest, softmax_total, summed)


def on_device(
    queries,
    prompt_key_cache,
    prompt_value_cache,
    kept,
    sample_keys,
    sample_values,
    suffix_len,
    decode_keys,
    decode_values,
    out_weight,
):
    seq_count = lax.axis_size("seq")
    seq_index = lax.axis_index("seq")
    own_count = queries.shape[1]
    step_count = queries.shape[2]
    head_count = queries.shape[3]
    head_dim = queries.shape[4]
    kv_count = prompt_key_cache.shape[1]
    group_size = head_count // kv_count
    logit_scale = 1.0 / math.sqrt(head_dim)
    gathered = lax.all_gather(queries, "seq", axis=1, tiled=True)
    sample_count = gathered.shape[1]
    grouped_queries = gathered[0].reshape(sample_count, step_count, kv_count, group_size, head_dim)
    query_rows = jnp.transpose(grouped_queries, (2, 0, 1, 3, 4)).reshape(
        kv_count, sample_count * step_count * group_size, head_dim
    )
    key_cache_store = prompt_key_cache[0].reshape(kv_count, KEPT_SLOTS, BLOCK_TOKENS, head_dim)
    value_cache_store = prompt_value_cache[0].reshape(kv_count, KEPT_SLOTS, BLOCK_TOKENS, head_dim)
    kept_block_counts = kept[0, :, 0]
    active_mask = jnp.arange(KEPT_SLOTS, dtype=jnp.int32)[None, :] < kept_block_counts[:, None]

    def one_head(pieces):
        head_row_block, key_block_list, value_block_list, live_blocks = pieces
        logit_scores = (
            jnp.einsum(
                "eg,mxg->emx", head_row_block, key_block_list, preferred_element_type=jnp.float32
            )
            * logit_scale
        )
        block_max = jnp.where(live_blocks[None, :], jnp.max(logit_scores, axis=2), NEGATIVE)
        attention_weights = jnp.where(
            live_blocks[None, :, None], jnp.exp(logit_scores - block_max[:, :, None]), 0.0
        )
        block_sum = jnp.sum(attention_weights, axis=2)
        block_output = jnp.einsum(
            "yaf,afi->yai",
            attention_weights.astype(jnp.bfloat16),
            value_block_list,
            preferred_element_type=jnp.float32,
        )
        highest = jnp.max(block_max, axis=1)
        factor = jnp.exp(block_max - highest[:, None])
        return (
            highest,
            jnp.sum(factor * block_sum, axis=1),
            jnp.sum(factor[:, :, None] * block_output, axis=1),
        )

    prompt_maximum, prompt_sum, prompt_output = lax.map(
        one_head, (query_rows, key_cache_store, value_cache_store, active_mask)
    )
    own_queries = queries[0].reshape(own_count, step_count, kv_count, group_size, head_dim)
    suffix_scores = (
        jnp.einsum(
            "nthgd,nhid->nhtgi", own_queries, sample_keys[0], preferred_element_type=jnp.float32
        )
        * logit_scale
    )
    fresh_scores = (
        jnp.einsum(
            "nthgd,nuhd->nhtgu", own_queries, decode_keys[0], preferred_element_type=jnp.float32
        )
        * logit_scale
    )
    position = jnp.arange(sample_keys.shape[3], dtype=jnp.int32)
    sample_token_mask = (position[None, :] < suffix_len[0][:, None])[:, None, None, None, :]
    step_index = jnp.arange(step_count, dtype=jnp.int32)
    newest_token_mask = (step_index[None, :] <= step_index[:, None])[None, None, :, None, :]
    tail_max = jnp.maximum(
        jnp.max(jnp.where(sample_token_mask, suffix_scores, NEGATIVE), axis=4),
        jnp.max(jnp.where(newest_token_mask, fresh_scores, NEGATIVE), axis=4),
    )
    suffix_weights = jnp.where(sample_token_mask, jnp.exp(suffix_scores - tail_max[..., None]), 0.0)
    fresh_weights = jnp.where(newest_token_mask, jnp.exp(fresh_scores - tail_max[..., None]), 0.0)
    tail_sum = jnp.sum(suffix_weights, axis=4) + jnp.sum(fresh_weights, axis=4)
    tail_out = jnp.einsum(
        "nhtgi,nhid->nhtgd",
        suffix_weights.astype(jnp.bfloat16),
        sample_values[0],
        preferred_element_type=jnp.float32,
    )
    tail_out = tail_out + jnp.einsum(
        "nhtgu,nuhd->nhtgd",
        fresh_weights.astype(jnp.bfloat16),
        decode_values[0],
        preferred_element_type=jnp.float32,
    )
    tail_part = (
        jnp.transpose(tail_max, (1, 0, 2, 3)),
        jnp.transpose(tail_sum, (1, 0, 2, 3)),
        jnp.transpose(tail_out, (1, 0, 2, 3, 4)),
    )
    prefix = (
        prompt_maximum.reshape(kv_count, sample_count, step_count, group_size),
        prompt_sum.reshape(kv_count, sample_count, step_count, group_size),
        prompt_output.reshape(kv_count, sample_count, step_count, group_size, head_dim),
    )
    offset = seq_index * own_count
    own_part = tuple((lax.dynamic_slice_in_dim(member, offset, own_count, 1) for member in prefix))
    merged = combine(own_part, tail_part)
    prefix = tuple(
        (
            lax.dynamic_update_slice_in_dim(member, update, offset, 1)
            for member, update in zip(prefix, merged)
        )
    )
    part_max = jnp.transpose(prefix[0], (1, 2, 0, 3)).reshape(sample_count, step_count, head_count)
    part_total = jnp.transpose(prefix[1], (1, 2, 0, 3)).reshape(
        sample_count, step_count, head_count
    )
    part_out = jnp.transpose(prefix[2], (1, 2, 0, 3, 4)).reshape(
        sample_count, step_count, head_count, head_dim
    )
    local_heads = head_count // seq_count
    highest, softmax_total, summed = joined((part_max, part_total, part_out), "seq", combine)
    highest = lax.dynamic_slice_in_dim(highest, seq_index * local_heads, local_heads, 2)
    softmax_total = lax.dynamic_slice_in_dim(softmax_total, seq_index * local_heads, local_heads, 2)
    summed = lax.dynamic_slice_in_dim(summed, seq_index * local_heads, local_heads, 2)
    head_out = (
        (summed / softmax_total[..., None])
        .astype(jnp.bfloat16)
        .reshape(sample_count * step_count, local_heads * head_dim)
    )
    all_rows = lax.all_gather(head_out, "prompt", axis=0, tiled=True)
    result = lax.psum_scatter(
        jnp.dot(all_rows, out_weight, preferred_element_type=jnp.float32),
        "seq",
        scatter_dimension=0,
        tiled=True,
    )
    return result.astype(jnp.bfloat16)


def solution(mesh):
    placed = (
        P("prompt", "seq", None, None, None),
        P("prompt", None, "seq", None),
        P("prompt", None, "seq", None),
        P("prompt", None, "seq"),
        P("prompt", "seq", None, None, None),
        P("prompt", "seq", None, None, None),
        P("prompt", "seq"),
        P("prompt", "seq", None, None, None),
        P("prompt", "seq", None, None, None),
        P("seq", "prompt"),
    )
    return jax.shard_map(
        on_device, mesh=mesh, in_specs=placed, out_specs=P("seq", "prompt"), check_vma=False
    )
```

profile of v0, /device:TPU:2, one launch (start us, length us, event | category | flops | bytes accessed | tf_op | source)
XLA Modules:
  0.0 388.6 jit_solution(14444092180296759480)
XLA Ops:
  8.0 27.6 %all_gather.15 = bf16[1,32,2,32,128]{4,3,2,0,1:T(8,128)(2,1)S(1)} all-gather(bf16[1,1,2,32,128]{4,3,2,0,1:T(8,128)(2,1)} %bitcast.184), channel_id=1, replica_groups=mesh['prompt'=16,'seq'=32] {'seq'}, dimensions={1}, use_global_device_ids=true | all-gather | bytes 540672 | tf_op jit(solution)/shard_map/all_gather | solution.py:52
  35.7 11.2 %while.33 = (s32[]{:T(128)}, f32[4,512]{1,0:T(4,128)S(1)}, f32[4,512]{1,0:T(4,128)S(1)}, f32[4,512,128]{2,1,0:T(8,128)S(1)}, pred[4,2]{1,0:T(4,128)(4,1)S(1)}, /...) while((s32[]{:T(128)}, f32[4,512]{1,0:T(4,128)S(1)}, ...), condition=%wide.region_6.7_spmd, body=%wide.region_0.6_spmd.sunk | while | flops 68356096 | bytes 3202187 | solution.py:90
  53.4 22.9 %all_gather.16 = f32[32,32,2,32]{3,1,2,0:T(8,128)S(1)} all-gather(f32[1,32,2,32]{3,1,2,0:T(8,128)S(1)} %copy.49), channel_id=1, replica_groups=mesh['prompt'=16,'seq'=32] {'seq'}, dimensions={0}, use_global_device_ids=true | all-gather | bytes 270336 | tf_op jit(solution)/shard_map/all_gather | solution.py:13
  76.4 24.8 %all_gather.17 = f32[32,32,2,32]{3,1,2,0:T(8,128)S(1)} all-gather(f32[1,32,2,32]{3,1,2,0:T(8,128)S(1)} %copy.53), channel_id=1, replica_groups=mesh['prompt'=16,'seq'=32] {'seq'}, dimensions={0}, use_global_device_ids=true | all-gather | bytes 270336 | tf_op jit(solution)/shard_map/all_gather | solution.py:13
  101.2 82.0 %all-gather.2.cloned.1.call-done = f32[32,32,2,32,128]{4,3,2,1,0:T(8,128)} async-done(((f32[1,32,2,32,128]{4,3,2,1,0:T(8,128)}), f32[32,32,2,32,128]{4,3,2,1,0:T(8,128)}) %all-gather.2.cloned.1.call-update) | async-done | bytes 33554448 | tf_op jit(solution)/shard_map/all_gather | solution.py:13
  184.5 63.3 %while.34 = (s32[]{:T(128)}, f32[32,2,32]{2,1,0:T(2,128)S(1)}, f32[32,2,32]{2,1,0:T(2,128)S(1)}, f32[32,2,32,128]{3,2,1,0:T(8,128)S(1)}, f32[32,32,2,32]{3,1,2,0...) while((s32[]{:T(128)}, f32[32,2,32]{2,1,0:T(2,128)S(1)}, ...), condition=%wide.region_12.13_spmd, body=%wide.region_11.12_spmd.sunk | while | flops 798725 | bytes 3260559 | solution.py:19
  184.6 1.9 fusion.72
  186.7 1.9 fusion.72
  188.7 1.9 fusion.72
  190.8 1.9 fusion.72
  192.8 1.9 fusion.72
  194.9 1.9 fusion.72
  196.9 1.9 fusion.72
  198.9 1.9 fusion.72
  201.0 1.9 fusion.72
  203.0 1.9 fusion.72
  205.1 1.9 fusion.72
  207.1 1.9 fusion.72
  209.2 1.9 fusion.72
  211.2 1.9 fusion.72
  213.2 1.9 fusion.72
  248.3 31.6 %all_gather.19 = bf16[1024,128]{1,0:T(8,128)(2,1)S(1)} all-gather(bf16[64,128]{1,0:T(8,128)(2,1)S(1)} %bitcast.185), channel_id=1, replica_groups=mesh['prompt'=16,'seq'=32] {'prompt'}, dimensions={0}, use_global_device_ids=true | all-gather | bytes 278528 | tf_op jit(solution)/shard_map/all_gather | solution.py:165
  279.9 2.7 fusion.51
  282.6 97.6 %reduce-scatter.2.cloned.1.call-done = f32[32,512]{1,0:T(8,128)} async-done(((f32[1024,512]{1,0:T(8,128)}), f32[32,512]{1,0:T(8,128)}) %reduce-scatter.2.cloned.1.call-update) | async-done | bytes 65552 | tf_op jit(solution)/shard_map/reduce_scatter | solution.py:166
  (158 shorter events, 55.4 us)
Async XLA Ops:
  6.5 41.6 %copy-start = (bf16[1,1,4,256,128]{4,3,2,1,0:T(8,128)(2,1)S(1)}, bf16[1,1,4,256,128]{4,3,2,1,0:T(8,128)(2,1)}, u32[]{:S(2)}) copy-start(bf16[1,1,4,256,128]{4,3,2,1,0:T(8,128)(2,1)} %param.18) | copy-start | bytes 786436
  6.5 176.7 %all-gather.2.cloned.1.call-start = ((), (), s32[]{:S(2)}) async-start(), calls=%async_computation.1 | async-start | bytes 34603008 | tf_op jit(solution)/shard_map/all_gather | solution.py:13
  53.0 327.3 %reduce-scatter.2.cloned.1.call-start = ((), (), s32[]{:S(2)}) async-start(), calls=%async_computation.2 | async-start | bytes 2162688 | tf_op jit(solution)/shard_map/reduce_scatter | solution.py:166
Sparse Core Ops, SparseCore 0:
  53.1 130.0 all-gather.1
  282.7 97.4 reduce-scatter.1
where the time goes:
time: 391 us; the launch traced here: 389 us
  waiting for transfers between devices  180 us (46%)
  blocking collectives  107 us (27%)
  other arithmetic  65.6 us (17%)
  matrix products  15.6 us (4%)
  between operations  14.2 us (4%)
  local copies, waits for them, and re-layouts  5.13 us (1%)
    reduce_scatter x1, waiting for transfers between devices, on_device(): lax.psum_scatter(jnp.dot(all_rows, out_weight, preferred_element_type=jnp...  97.6 us
    all_gather x1, waiting for transfers between devices, joined(): everything = jax.tree.map(lambda part: lax.all_gather(part, axis), x)  82 us
    add x31, other arithmetic, combine(): earlier[2] * early_factor[..., None] + later[2] * late_factor[..., None]  58.6 us
    all_gather x2, blocking collectives, joined(): everything = jax.tree.map(lambda part: lax.all_gather(part, axis), x)  47.8 us
    all_gather x1, blocking collectives, on_device(): all_rows = lax.all_gather(head_out, 'prompt', axis=0, tiled=True)  31.6 us
    all_gather x1, blocking collectives, on_device(): gathered = lax.all_gather(queries, 'seq', axis=1, tiled=True)  27.6 us
  transfers between devices with their start and end apart: 2, of which 2 were waited for; matrix products, arithmetic and copies ran while one was open for 0% of the time, Pallas kernels for 0%

commit v1 on v0

--- a/solution.py
+++ b/solution.py
@@ -162,7 +162,24 @@
         .astype(jnp.bfloat16)
         .reshape(sample_count * step_count, local_heads * head_dim)
     )
-    all_rows = lax.all_gather(head_out, "prompt", axis=0, tiled=True)
+    ways, here, step = (lax.axis_size("prompt"), lax.axis_index("prompt"), head_out.shape[0])
+    dims = [n * ways if d == 0 else n for d, n in enumerate(head_out.shape)]
+    all_rows = lax.dynamic_update_slice_in_dim(
+        jnp.zeros(dims, head_out.dtype), head_out, here * step, axis=0
+    )
+    going_up = going_down = head_out
+    for far in range(1, ways // 2 + 1):
+        going_up = lax.ppermute(going_up, "prompt", [(d, (d + 1) % ways) for d in range(ways)])
+        all_rows = lax.dynamic_update_slice_in_dim(
+            all_rows, going_up, (here - far) % ways * step, axis=0
+        )
+        if 2 * far < ways:
+            going_down = lax.ppermute(
+                going_down, "prompt", [(d, (d - 1) % ways) for d in range(ways)]
+            )
+            all_rows = lax.dynamic_update_slice_in_dim(
+                all_rows, going_down, (here + far) % ways * step, axis=0
+            )
     result = lax.psum_scatter(
         jnp.dot(all_rows, out_weight, preferred_element_type=jnp.float32),
         "seq",

time: 391 us -> 420 us (1.074)
  starting transfers between devices: 0.04 us -> 52.2 us
  blocking collectives: 107 us -> 75.7 us
  waiting for transfers between devices: 180 us -> 187 us
    ppermute x0 -> x15, starting transfers between devices: none -> 52.1 us  [the longest x7 35.2 us: on_device(): lax.ppermute(going_down, 'prompt', [(d, (d - 1) % ways) for d in range(wa...]
    all_gather x1 -> x0, blocking collectives: 31.6 us -> none  [on_device(): all_rows = lax.all_gather(head_out, 'prompt', axis=0, tiled=True)]
    ppermute x0 -> x15, waiting for transfers between devices: none -> 4.91 us  [the longest x8 4.89 us: on_device(): lax.ppermute(going_up, 'prompt', [(d, (d + 1) % ways) for d in range(ways)])]
  transfers between devices with their start and end apart: 2 -> 17, of which waited for: 2 -> 3; matrix products, arithmetic and copies ran while one was open for 0% -> 0% of each run, Pallas kernels for 0% -> 0%
where the time goes in v1:
time: 420 us; the launch traced here: 417 us
  waiting for transfers between devices  187 us (45%)
  blocking collectives  75.7 us (18%)
  other arithmetic  65.6 us (16%)
  starting transfers between devices  52.2 us (12%)
  matrix products  15.6 us (4%)
  between operations  14.8 us (4%)
  local copies, waits for them, and re-layouts  5.43 us (1%)
    reduce_scatter x1, waiting for transfers between devices, on_device(): lax.psum_scatter(jnp.dot(all_rows, out_weight, preferred_element_type=jnp...  100 us
    all_gather x1, waiting for transfers between devices, joined(): everything = jax.tree.map(lambda part: lax.all_gather(part, axis), x)  81.4 us
    add x31, other arithmetic, combine(): earlier[2] * early_factor[..., None] + later[2] * late_factor[..., None]  58.6 us
    all_gather x2, blocking collectives, joined(): everything = jax.tree.map(lambda part: lax.all_gather(part, axis), x)  47.9 us
    ppermute x7, starting transfers between devices, on_device(): lax.ppermute(going_down, 'prompt', [(d, (d - 1) % ways) for d in range(wa...  35.2 us
    all_gather x1, blocking collectives, on_device(): gathered = lax.all_gather(queries, 'seq', axis=1, tiled=True)  27.8 us
    ppermute x8, starting transfers between devices, on_device(): lax.ppermute(going_up, 'prompt', [(d, (d + 1) % ways) for d in range(ways)])  16.9 us
  transfers between devices with their start and end apart: 17, of which 3 were waited for; matrix products, arithmetic and copies ran while one was open for 0% of the time, Pallas kernels for 0%

profile of v1, /device:TPU:2, one launch (start us, length us, event | category | flops | bytes accessed | tf_op | source)
XLA Modules:
  0.0 417.2 jit_solution(3367016709007059453)
XLA Ops:
  6.6 27.8 %all_gather.12 = bf16[1,32,2,32,128]{4,3,2,0,1:T(8,128)(2,1)S(1)} all-gather(bf16[1,1,2,32,128]{4,3,2,0,1:T(8,128)(2,1)} %bitcast.182), channel_id=1, replica_groups=mesh['prompt'=16,'seq'=32] {'seq'}, dimensions={1}, use_global_device_ids=true | all-gather | bytes 540672 | tf_op jit(solution)/shard_map/all_gather | solution.py:52
  35.2 11.2 %while.33 = (s32[]{:T(128)}, f32[4,512]{1,0:T(4,128)S(1)}, f32[4,512]{1,0:T(4,128)S(1)}, f32[4,512,128]{2,1,0:T(8,128)S(1)}, pred[4,2]{1,0:T(4,128)(4,1)S(1)}, /...) while((s32[]{:T(128)}, f32[4,512]{1,0:T(4,128)S(1)}, ...), condition=%wide.region_6.7_spmd, body=%wide.region_0.6_spmd.sunk | while | flops 68356096 | bytes 3202687 | solution.py:90
  53.5 23.0 %all_gather.13 = f32[32,32,2,32]{3,1,2,0:T(8,128)S(1)} all-gather(f32[1,32,2,32]{3,1,2,0:T(8,128)S(1)} %copy.49), channel_id=1, replica_groups=mesh['prompt'=16,'seq'=32] {'seq'}, dimensions={0}, use_global_device_ids=true | all-gather | bytes 270336 | tf_op jit(solution)/shard_map/all_gather | solution.py:13
  76.7 24.9 %all_gather.14 = f32[32,32,2,32]{3,1,2,0:T(8,128)S(1)} all-gather(f32[1,32,2,32]{3,1,2,0:T(8,128)S(1)} %copy.53), channel_id=1, replica_groups=mesh['prompt'=16,'seq'=32] {'seq'}, dimensions={0}, use_global_device_ids=true | all-gather | bytes 270336 | tf_op jit(solution)/shard_map/all_gather | solution.py:13
  101.7 81.4 %all-gather.2.cloned.1.call-done = f32[32,32,2,32,128]{4,3,2,1,0:T(8,128)} async-done(((f32[1,32,2,32,128]{4,3,2,1,0:T(8,128)}), f32[32,32,2,32,128]{4,3,2,1,0:T(8,128)}) %all-gather.2.cloned.1.call-update) | async-done | bytes 33554448 | tf_op jit(solution)/shard_map/all_gather | solution.py:13
  184.4 63.4 %while.34 = (s32[]{:T(128)}, f32[32,2,32]{2,1,0:T(2,128)S(1)}, f32[32,2,32]{2,1,0:T(2,128)S(1)}, f32[32,2,32,128]{3,2,1,0:T(8,128)S(1)}, f32[32,32,2,32]{3,1,2,0...) while((s32[]{:T(128)}, f32[32,2,32]{2,1,0:T(2,128)S(1)}, ...), condition=%wide.region_12.13_spmd, body=%wide.region_11.12_spmd.sunk | while | flops 798725 | bytes 3260567 | solution.py:19
  248.3 3.5 collective-permute-start
  251.8 4.4 %collective-permute-start.1 = (bf16[64,128]{1,0:T(8,128)(2,1)S(1)}, bf16[64,128]{1,0:T(8,128)(2,1)S(1)}, u32[]{:S(2)}, u32[]{:S(2)}) collective-permute-start(bf16[64,128]{1,0:T(8,128)(2,1)S(1)} %bitcast.184), channel_id=1, source_target_pairs={{0,480},{32,0},{64,32},{96,64},{128,96},{160,128},{192,160},{224,1... | collective-permute-start | bytes 49160 | tf_op jit(solution)/shard_map/ppermute | solution.py:177
  256.2 1.9 collective-permute-start.2
  258.2 5.1 %collective-permute-start.3 = (bf16[64,128]{1,0:T(8,128)(2,1)S(1)}, bf16[64,128]{1,0:T(8,128)(2,1)S(1)}, u32[]{:S(2)}, u32[]{:S(2)}) collective-permute-start(bf16[64,128]{1,0:T(8,128)(2,1)S(1)} %collective-permute-done.1), channel_id=1, source_target_pairs={{0,480},{32,0},{64,32},{96,64},{128,96},{160,128},{192,160},{224,1... | collective-permute-start | bytes 49160 | tf_op jit(solution)/shard_map/ppermute | solution.py:177
  263.4 1.9 collective-permute-start.4
  265.3 5.1 %collective-permute-start.5 = (bf16[64,128]{1,0:T(8,128)(2,1)S(1)}, bf16[64,128]{1,0:T(8,128)(2,1)S(1)}, u32[]{:S(2)}, u32[]{:S(2)}) collective-permute-start(bf16[64,128]{1,0:T(8,128)(2,1)S(1)} %collective-permute-done.3), channel_id=1, source_target_pairs={{0,480},{32,0},{64,32},{96,64},{128,96},{160,128},{192,160},{224,1... | collective-permute-start | bytes 49160 | tf_op jit(solution)/shard_map/ppermute | solution.py:177
  270.5 1.9 collective-permute-start.6
  272.4 5.1 %collective-permute-start.7 = (bf16[64,128]{1,0:T(8,128)(2,1)S(1)}, bf16[64,128]{1,0:T(8,128)(2,1)S(1)}, u32[]{:S(2)}, u32[]{:S(2)}) collective-permute-start(bf16[64,128]{1,0:T(8,128)(2,1)S(1)} %collective-permute-done.5), channel_id=1, source_target_pairs={{0,480},{32,0},{64,32},{96,64},{128,96},{160,128},{192,160},{224,1... | collective-permute-start | bytes 49160 | tf_op jit(solution)/shard_map/ppermute | solution.py:177
  277.6 1.9 collective-permute-start.8
  279.6 5.1 %collective-permute-start.9 = (bf16[64,128]{1,0:T(8,128)(2,1)S(1)}, bf16[64,128]{1,0:T(8,128)(2,1)S(1)}, u32[]{:S(2)}, u32[]{:S(2)}) collective-permute-start(bf16[64,128]{1,0:T(8,128)(2,1)S(1)} %collective-permute-done.7), channel_id=1, source_target_pairs={{0,480},{32,0},{64,32},{96,64},{128,96},{160,128},{192,160},{224,1... | collective-permute-start | bytes 49160 | tf_op jit(solution)/shard_map/ppermute | solution.py:177
  284.7 1.9 collective-permute-start.10
  286.7 5.1 %collective-permute-start.11 = (bf16[64,128]{1,0:T(8,128)(2,1)S(1)}, bf16[64,128]{1,0:T(8,128)(2,1)S(1)}, u32[]{:S(2)}, u32[]{:S(2)}) collective-permute-start(bf16[64,128]{1,0:T(8,128)(2,1)S(1)} %collective-permute-done.9), channel_id=1, source_target_pairs={{0,480},{32,0},{64,32},{96,64},{128,96},{160,128},{192,160},{224,1... | collective-permute-start | bytes 49160 | tf_op jit(solution)/shard_map/ppermute | solution.py:177
  291.9 1.9 collective-permute-start.12
  293.8 5.1 %collective-permute-start.13 = (bf16[64,128]{1,0:T(8,128)(2,1)S(1)}, bf16[64,128]{1,0:T(8,128)(2,1)S(1)}, u32[]{:S(2)}, u32[]{:S(2)}) collective-permute-start(bf16[64,128]{1,0:T(8,128)(2,1)S(1)} %collective-permute-done.11), channel_id=1, source_target_pairs={{0,480},{32,0},{64,32},{96,64},{128,96},{160,128},{192,160},{224,1... | collective-permute-start | bytes 49160 | tf_op jit(solution)/shard_map/ppermute | solution.py:177
  299.0 1.9 collective-permute-start.14
  301.0 4.9 %collective-permute-done.14 = bf16[64,128]{1,0:T(8,128)(2,1)S(1)} collective-permute-done((bf16[64,128]{1,0:T(8,128)(2,1)S(1)}, bf16[64,128]{1,0:T(8,128)(2,1)S(1)}, u32[]{:S(2)}, u32[]{:S(2)}) %collective-permute-start.14) | collective-permute-done | bytes 16416 | tf_op jit(solution)/shard_map/ppermute | solution.py:172
  305.9 2.7 fusion.51
  308.5 100.4 %reduce-scatter.2.cloned.1.call-done = f32[32,512]{1,0:T(8,128)} async-done(((f32[1024,512]{1,0:T(8,128)}), f32[32,512]{1,0:T(8,128)}) %reduce-scatter.2.cloned.1.call-update) | async-done | bytes 65552 | tf_op jit(solution)/shard_map/reduce_scatter | solution.py:183
  (204 shorter events, 84.1 us)
Async XLA Ops:
  6.5 40.8 %copy-start = (bf16[1,1,4,256,128]{4,3,2,1,0:T(8,128)(2,1)S(1)}, bf16[1,1,4,256,128]{4,3,2,1,0:T(8,128)(2,1)}, u32[]{:S(2)}) copy-start(bf16[1,1,4,256,128]{4,3,2,1,0:T(8,128)(2,1)} %param.18) | copy-start | bytes 786436
  6.5 176.6 %all-gather.2.cloned.1.call-start = ((), (), s32[]{:S(2)}) async-start(), calls=%async_computation.1 | async-start | bytes 34603008 | tf_op jit(solution)/shard_map/all_gather | solution.py:13
  53.1 355.9 %reduce-scatter.2.cloned.1.call-start = ((), (), s32[]{:S(2)}) async-start(), calls=%async_computation.2 | async-start | bytes 2162688 | tf_op jit(solution)/shard_map/reduce_scatter | solution.py:183
  248.3 8.0 %collective-permute-start = (bf16[64,128]{1,0:T(8,128)(2,1)S(1)}, bf16[64,128]{1,0:T(8,128)(2,1)S(1)}, u32[]{:S(2)}, u32[]{:S(2)}) collective-permute-start(bf16[64,128]{1,0:T(8,128)(2,1)S(1)} %bitcast.183), channel_id=1, source_target_pairs={{0,32},{32,64},{64,96},{96,128},{128,160},{160,192},{192,224},{224... | collective-permute-start | bytes 49160 | tf_op jit(solution)/shard_map/ppermute | solution.py:172
  251.8 6.4 %collective-permute-start.1 = (bf16[64,128]{1,0:T(8,128)(2,1)S(1)}, bf16[64,128]{1,0:T(8,128)(2,1)S(1)}, u32[]{:S(2)}, u32[]{:S(2)}) collective-permute-start(bf16[64,128]{1,0:T(8,128)(2,1)S(1)} %bitcast.184), channel_id=1, source_target_pairs={{0,480},{32,0},{64,32},{96,64},{128,96},{160,128},{192,160},{224,1... | collective-permute-start | bytes 49160 | tf_op jit(solution)/shard_map/ppermute | solution.py:177
  256.2 7.1 %collective-permute-start.2 = (bf16[64,128]{1,0:T(8,128)(2,1)S(1)}, bf16[64,128]{1,0:T(8,128)(2,1)S(1)}, u32[]{:S(2)}, u32[]{:S(2)}) collective-permute-start(bf16[64,128]{1,0:T(8,128)(2,1)S(1)} %collective-permute-done), channel_id=1, source_target_pairs={{0,32},{32,64},{64,96},{96,128},{128,160},{160,192},{192,224},{224... | collective-permute-start | bytes 49160 | tf_op jit(solution)/shard_map/ppermute | solution.py:172
  258.2 7.1 %collective-permute-start.3 = (bf16[64,128]{1,0:T(8,128)(2,1)S(1)}, bf16[64,128]{1,0:T(8,128)(2,1)S(1)}, u32[]{:S(2)}, u32[]{:S(2)}) collective-permute-start(bf16[64,128]{1,0:T(8,128)(2,1)S(1)} %collective-permute-done.1), channel_id=1, source_target_pairs={{0,480},{32,0},{64,32},{96,64},{128,96},{160,128},{192,160},{224,1... | collective-permute-start | bytes 49160 | tf_op jit(solution)/shard_map/ppermute | solution.py:177
  263.4 7.1 %collective-permute-start.4 = (bf16[64,128]{1,0:T(8,128)(2,1)S(1)}, bf16[64,128]{1,0:T(8,128)(2,1)S(1)}, u32[]{:S(2)}, u32[]{:S(2)}) collective-permute-start(bf16[64,128]{1,0:T(8,128)(2,1)S(1)} %collective-permute-done.2), channel_id=1, source_target_pairs={{0,32},{32,64},{64,96},{96,128},{128,160},{160,192},{192,224},{224... | collective-permute-start | bytes 49160 | tf_op jit(solution)/shard_map/ppermute | solution.py:172
  265.3 7.1 %collective-permute-start.5 = (bf16[64,128]{1,0:T(8,128)(2,1)S(1)}, bf16[64,128]{1,0:T(8,128)(2,1)S(1)}, u32[]{:S(2)}, u32[]{:S(2)}) collective-permute-start(bf16[64,128]{1,0:T(8,128)(2,1)S(1)} %collective-permute-done.3), channel_id=1, source_target_pairs={{0,480},{32,0},{64,32},{96,64},{128,96},{160,128},{192,160},{224,1... | collective-permute-start | bytes 49160 | tf_op jit(solution)/shard_map/ppermute | solution.py:177
  270.5 7.1 %collective-permute-start.6 = (bf16[64,128]{1,0:T(8,128)(2,1)S(1)}, bf16[64,128]{1,0:T(8,128)(2,1)S(1)}, u32[]{:S(2)}, u32[]{:S(2)}) collective-permute-start(bf16[64,128]{1,0:T(8,128)(2,1)S(1)} %collective-permute-done.4), channel_id=1, source_target_pairs={{0,32},{32,64},{64,96},{96,128},{128,160},{160,192},{192,224},{224... | collective-permute-start | bytes 49160 | tf_op jit(solution)/shard_map/ppermute | solution.py:172
  272.4 7.1 %collective-permute-start.7 = (bf16[64,128]{1,0:T(8,128)(2,1)S(1)}, bf16[64,128]{1,0:T(8,128)(2,1)S(1)}, u32[]{:S(2)}, u32[]{:S(2)}) collective-permute-start(bf16[64,128]{1,0:T(8,128)(2,1)S(1)} %collective-permute-done.5), channel_id=1, source_target_pairs={{0,480},{32,0},{64,32},{96,64},{128,96},{160,128},{192,160},{224,1... | collective-permute-start | bytes 49160 | tf_op jit(solution)/shard_map/ppermute | solution.py:177
  277.6 7.1 %collective-permute-start.8 = (bf16[64,128]{1,0:T(8,128)(2,1)S(1)}, bf16[64,128]{1,0:T(8,128)(2,1)S(1)}, u32[]{:S(2)}, u32[]{:S(2)}) collective-permute-start(bf16[64,128]{1,0:T(8,128)(2,1)S(1)} %collective-permute-done.6), channel_id=1, source_target_pairs={{0,32},{32,64},{64,96},{96,128},{128,160},{160,192},{192,224},{224... | collective-permute-start | bytes 49160 | tf_op jit(solution)/shard_map/ppermute | solution.py:172
  279.6 7.1 %collective-permute-start.9 = (bf16[64,128]{1,0:T(8,128)(2,1)S(1)}, bf16[64,128]{1,0:T(8,128)(2,1)S(1)}, u32[]{:S(2)}, u32[]{:S(2)}) collective-permute-start(bf16[64,128]{1,0:T(8,128)(2,1)S(1)} %collective-permute-done.7), channel_id=1, source_target_pairs={{0,480},{32,0},{64,32},{96,64},{128,96},{160,128},{192,160},{224,1... | collective-permute-start | bytes 49160 | tf_op jit(solution)/shard_map/ppermute | solution.py:177
  284.7 7.1 %collective-permute-start.10 = (bf16[64,128]{1,0:T(8,128)(2,1)S(1)}, bf16[64,128]{1,0:T(8,128)(2,1)S(1)}, u32[]{:S(2)}, u32[]{:S(2)}) collective-permute-start(bf16[64,128]{1,0:T(8,128)(2,1)S(1)} %collective-permute-done.8), channel_id=1, source_target_pairs={{0,32},{32,64},{64,96},{96,128},{128,160},{160,192},{192,224},{224... | collective-permute-start | bytes 49160 | tf_op jit(solution)/shard_map/ppermute | solution.py:172
  286.7 7.1 %collective-permute-start.11 = (bf16[64,128]{1,0:T(8,128)(2,1)S(1)}, bf16[64,128]{1,0:T(8,128)(2,1)S(1)}, u32[]{:S(2)}, u32[]{:S(2)}) collective-permute-start(bf16[64,128]{1,0:T(8,128)(2,1)S(1)} %collective-permute-done.9), channel_id=1, source_target_pairs={{0,480},{32,0},{64,32},{96,64},{128,96},{160,128},{192,160},{224,1... | collective-permute-start | bytes 49160 | tf_op jit(solution)/shard_map/ppermute | solution.py:177
  291.9 7.1 %collective-permute-start.12 = (bf16[64,128]{1,0:T(8,128)(2,1)S(1)}, bf16[64,128]{1,0:T(8,128)(2,1)S(1)}, u32[]{:S(2)}, u32[]{:S(2)}) collective-permute-start(bf16[64,128]{1,0:T(8,128)(2,1)S(1)} %collective-permute-done.10), channel_id=1, source_target_pairs={{0,32},{32,64},{64,96},{96,128},{128,160},{160,192},{192,224},{224... | collective-permute-start | bytes 49160 | tf_op jit(solution)/shard_map/ppermute | solution.py:172
  293.8 7.1 %collective-permute-start.13 = (bf16[64,128]{1,0:T(8,128)(2,1)S(1)}, bf16[64,128]{1,0:T(8,128)(2,1)S(1)}, u32[]{:S(2)}, u32[]{:S(2)}) collective-permute-start(bf16[64,128]{1,0:T(8,128)(2,1)S(1)} %collective-permute-done.11), channel_id=1, source_target_pairs={{0,480},{32,0},{64,32},{96,64},{128,96},{160,128},{192,160},{224,1... | collective-permute-start | bytes 49160 | tf_op jit(solution)/shard_map/ppermute | solution.py:177
  299.0 6.8 %collective-permute-start.14 = (bf16[64,128]{1,0:T(8,128)(2,1)S(1)}, bf16[64,128]{1,0:T(8,128)(2,1)S(1)}, u32[]{:S(2)}, u32[]{:S(2)}) collective-permute-start(bf16[64,128]{1,0:T(8,128)(2,1)S(1)} %collective-permute-done.12), channel_id=1, source_target_pairs={{0,32},{32,64},{64,96},{96,128},{128,160},{160,192},{192,224},{224... | collective-permute-start | bytes 49160 | tf_op jit(solution)/shard_map/ppermute | solution.py:172
Sparse Core Ops, SparseCore 0:
  53.2 129.8 all-gather.1
  308.7 100.2 reduce-scatter.1
